TPU v7x, 128 devices: a whole 4x4x4 slice. The times are simulated.
128 devices in a mesh: gx: 16 (over y, z), gy: 8 (over x, core).
Axes of the slice: x: 4, y: 4, z: 4, core: 2. Of those that a mesh axis runs over, the one named last changes fastest.
Arguments:
- soil_field: float32 [128, 64, 4, 256], P('gx', 'gy'), may hold values from 0 to 3
- rhizosphere: float32 [32768, 4, 128], P(('gx', 'gy')), may hold values from 0 to 1
- conductance: float32 [32768, 4, 128], P(('gx', 'gy')), may hold values from 0.02 to 0.45
- uptake_rate: float32 [32768, 4], P(('gx', 'gy')), may hold values from 0.02 to 0.45
- segment_weight: float32 [32768, 256], P(('gx', 'gy')), may hold values from 0.1 to 1
- segment_target: int32 [32768, 1], P(('gx', 'gy')), may hold values from 0 to 127; in each aligned block of 256 rows (0 to 255, 256 to 511, ...) at most 3 rows name the same one
- segment_tile: int32 [32768], P(('gx', 'gy')), may hold values from 0 to 63
- segment_count: int32 [128], P(('gx', 'gy')), may hold values from 1 to 256, 19660 in all
Outputs:
- rhizosphere_next: float32 [32768, 4, 128], P(('gx', 'gy'))
- soil_sink: float32 [128, 64, 4, 256], P('gx', 'gy')
Inputs may be any that keep to these rules, and one draw needn't show every extreme that they name: `segment_target`: among the segment slots of one device no device is named by more than 3 slots, and some device is named by exactly 3. `segment_count`: some device has all 256 slots live.
All inputs are finite; a program needn't handle non-finite values.
Results may differ from a plain program's by a relative error of at most 0.00005.
Values sent between devices are 32-bit elements; how exact they have to be, the bound alone decides.
A program may use at most 128 MiB of HBM per device.

v0:
```python
import jax
import jax.numpy as jnp
from jax import lax
from jax.sharding import PartitionSpec as P

SUB = 32


def radial_steps(profile, conductance, uptake_rate, boundary):

    def substep(step, state_pair):
        level, drawn = state_pair
        outward = jnp.concatenate([level[:, :, 1:], boundary[:, :, None]], axis=2)
        current = conductance * (outward - level)
        absorbed = uptake_rate[:, :, None] * level[:, :, :1]
        incoming = jnp.concatenate([absorbed, current[:, :, :-1]], axis=2)
        return (level + current - incoming, drawn + current[:, :, -1])

    start = (profile, jnp.zeros(profile.shape[:2], jnp.float32))
    return lax.fori_loop(0, SUB, substep, start)


def route_requests(wanted):
    return lax.all_to_all(wanted, ("gx", "gy"), split_axis=0, concat_axis=0, tiled=True)


def route_values(served):
    return lax.all_to_all(served, ("gx", "gy"), split_axis=0, concat_axis=0, tiled=True)


def route_uptake(wanted, uptake_rows):
    return (
        lax.all_to_all(wanted, ("gx", "gy"), split_axis=0, concat_axis=0, tiled=True),
        lax.all_to_all(uptake_rows, ("gx", "gy"), split_axis=0, concat_axis=0, tiled=True),
    )


def on_device(
    soil_field,
    rhizosphere,
    conductance,
    uptake_rate,
    segment_weight,
    segment_target,
    segment_tile,
    segment_count,
):
    peers = lax.axis_size(("gx", "gy"))
    segments = rhizosphere.shape[0]
    fields = soil_field.shape[2]
    voxels = soil_field.shape[3]
    tiles_count = soil_field.shape[0] * soil_field.shape[1]
    capacity = segments * 3 // (2 * peers)
    slot_total = peers * capacity
    active = jnp.arange(segments, dtype=jnp.int32) < segment_count[0]
    target = segment_target[:, 0]
    matches = (
        (target[:, None] == jnp.arange(peers, dtype=jnp.int32)[None, :]) & active[:, None]
    ).astype(jnp.int32)
    position = jnp.sum(jnp.where(matches > 0, jnp.cumsum(matches, axis=0) - 1, 0), axis=1)
    placement = jnp.where(active, target * capacity + position, slot_total)
    wanted = (
        jnp.full((slot_total,), tiles_count, jnp.int32).at[placement].set(segment_tile, mode="drop")
    )
    wanted = wanted.reshape(peers, capacity)
    slot_source = (
        jnp.full((slot_total,), segments, jnp.int32)
        .at[placement]
        .set(jnp.arange(segments, dtype=jnp.int32), mode="drop")
    )
    slot_used = slot_source < segments
    slot_index = jnp.minimum(slot_source, segments - 1)
    soil_tiles = soil_field.reshape(tiles_count, fields, voxels)
    requested = route_requests(wanted)
    served = jnp.take(soil_tiles, jnp.minimum(requested, tiles_count - 1).reshape(-1), axis=0)
    returned = route_values(served.reshape(peers, capacity, fields, voxels))
    gathered = jnp.take(
        returned.reshape(slot_total, fields, voxels), jnp.minimum(placement, slot_total - 1), axis=0
    )
    weight_total = jnp.sum(segment_weight, axis=1)
    boundary = (
        jnp.einsum("sfv,sv->sf", gathered, segment_weight, precision=lax.Precision.HIGHEST)
        / weight_total[:, None]
    )
    boundary = jnp.where(active[:, None], boundary, 0.0)
    profile, drawn = radial_steps(rhizosphere, conductance, uptake_rate, boundary)
    rhizosphere_next = jnp.where(active[:, None, None], profile, rhizosphere)
    drawn = jnp.where(active[:, None], drawn, 0.0)
    portion = segment_weight / weight_total[:, None]
    slot_drawn = jnp.where(slot_used[:, None], jnp.take(drawn, slot_index, axis=0), 0.0)
    slot_portion = jnp.take(portion, slot_index, axis=0)
    outgoing = slot_drawn[:, :, None] * slot_portion[:, None, :]
    arrived_ids, arrived_rows = route_uptake(
        wanted, outgoing.reshape(peers, capacity, fields, voxels)
    )
    selector = (
        arrived_ids.reshape(-1)[None, :] == jnp.arange(tiles_count, dtype=jnp.int32)[:, None]
    ).astype(jnp.float32)
    collected = jnp.dot(
        selector,
        arrived_rows.reshape(slot_total, fields * voxels),
        precision=lax.Precision.HIGHEST,
        preferred_element_type=jnp.float32,
    )
    soil_sink = collected.reshape(soil_field.shape[0], soil_field.shape[1], fields, voxels)
    return (rhizosphere_next, soil_sink)


def solution(mesh):
    return jax.shard_map(
        on_device,
        mesh=mesh,
        in_specs=(
            P("gx", "gy", None, None),
            P(("gx", "gy"), None, None),
            P(("gx", "gy"), None, None),
            P(("gx", "gy"), None),
            P(("gx", "gy"), None),
            P(("gx", "gy"), None),
            P(("gx", "gy")),
            P(("gx", "gy")),
        ),
        out_specs=(P(("gx", "gy"), None, None), P("gx", "gy", None, None)),
        check_vma=False,
    )
```

profile of v0, /device:TPU:1, one launch (start us, length us, event | category | flops | bytes accessed | tf_op | source)
XLA Modules:
  0.0 187.7 jit_solution(65044457631634833)
XLA Ops:
  1.4 0.8 copy.55
  2.6 0.9 fusion.7
  3.5 0.7 and_reduce_fusion
  4.2 1.6 scatter_custom_fusion
  6.0 20.8 %all_to_all.23 = s32[128,1,3]{2,1,0:T(1,128)S(1)} all-to-all(s32[128,1,3]{2,1,0:T(1,128)S(1)} %bitcast.59), channel_id=1, replica_groups=mesh['gx'=16,'gy'=8] {'gx','gy'}, dimensions={0} | all-to-all | bytes 3072 | tf_op jit(solution)/shard_map/all_to_all | solution.py:24
  26.8 0.5 broadcast.212
  27.3 1.0 fusion.24
  28.6 2.5 %gather_fusion = f32[384,4,256]{2,1,0:T(4,128)S(1)} fusion(f32[64,4,256]{2,1,0:T(4,128)S(1)} %bitcast.51, s32[1024]{0:T(1024)S(1)} %pad_clamp_fusion.2), kind=kCustom, calls=%fused_computation | custom fusion | bytes 3147264 | tf_op jit(solution)/shard_map/jit(_take)/gather | solution.py:75
  31.1 1.5 broadcast_select_fusion
  32.6 4.6 %all-to-all-start.1 = ((f32[128,3,4,256]{3,2,1,0:T(4,128)}), f32[128,3,4,256]{3,2,1,0:T(4,128)S(1)}, u32[]{:S(2)}, u32[]{:S(2)}) async-start(f32[128,3,4,256]{3,2,1,0:T(4,128)} %broadcast_select_fusion), calls=%async_computation.1 | async-start | bytes 3145728 | tf_op jit(solution)/shard_map/all_to_all | solution.py:28
  37.5 1.3 copy.60
  38.8 1.6 scatter_custom_fusion.1
  41.1 2.2 %gather_fusion.3 = f32[384,256]{1,0:T(8,128)} fusion(f32[256,256]{1,0:T(8,128)S(1)} %broadcast_divide_fusion, s32[1024]{0:T(1024)S(1)} %pad_clamp_fusion), kind=kCustom, calls=%fused_computation.3 | custom fusion | bytes 787968 | tf_op jit(solution)/shard_map/jit(_take)/gather | solution.py:91
  43.3 1.2 gather.28
  44.5 1.0 broadcast_select_fusion.1
  45.5 16.6 %all-to-all-done.1 = f32[128,3,4,256]{3,2,1,0:T(4,128)S(1)} async-done(((f32[128,3,4,256]{3,2,1,0:T(4,128)}), f32[128,3,4,256]{3,2,1,0:T(4,128)S(1)}, u32[]{:S(2)}, u32[]{:S(2)}) %all-to-all-start.1) | async-done | bytes 1572896 | tf_op jit(solution)/shard_map/all_to_all | solution.py:28
  62.1 2.2 %gather_fusion.1 = f32[256,4,256]{2,1,0:T(4,128)} fusion(f32[384,4,256]{2,1,0:T(4,128)S(1)} %bitcast.57, s32[1024]{0:T(1024)S(1)} %pad_clamp_fusion.1), kind=kCustom, calls=%fused_computation.1 | custom fusion | bytes 2098176 | tf_op jit(solution)/shard_map/jit(_take)/gather | solution.py:77
  64.3 3.5 %fusion.1 = f32[256,1,4]{2,1,0:T(1,128)S(1)} fusion(f32[256,4,256]{2,1,0:T(4,128)} %gather_fusion.1, pred[256]{0:T(512)(128)(4,1)S(1)} %get-tuple-element.122, f32[256,256,1]{1,0,2:T(8,128)S(1)} %bitcast.58), kind=kOutput, calls=%fused_computation.12 | convolution fusion | flops 3407872 | bytes 1315072 | tf_op jit(solution)/shard_map/sfv,sv->sf/dot_general | solution.py:82
  68.0 80.8 %while.13 = (s32[]{:T(128)}, f32[256,4,128]{0,1,2:T(4,128)S(1)}, f32[256,4]{0,1:T(4,128)S(1)}, f32[256,4]{0,1:T(4,128)S(1)}, f32[256,4,128]{0,1,2:T(4,128)S(1)}, /*index=5*/f32[256,4]{0,1:T(4,128)S(1)}, s32[]{:T(128)}, s32[]{:T(128)}) while((s32[]{:T(128)}, f32[256,4,128]{0,1,2:T(4,128)S(1)}, f32[256,4]{0,1:T(4,128)S(1)}, ...), condition=%wide.region_6.7_spmd.clone, body=%wide.region_5.6_spmd.clone.sunk | while | flops 789507 | bytes 12624023 | solution.py:20
  72.5 0.4 slice_reduce_fusion.2
  75.0 0.4 slice_reduce_fusion.2
  77.6 0.4 slice_reduce_fusion.2
  80.1 0.4 slice_reduce_fusion.2
  87.7 0.4 slice_reduce_fusion.2
  90.2 0.4 slice_reduce_fusion.2
  92.7 0.4 slice_reduce_fusion.2
  95.2 0.4 slice_reduce_fusion.2
  105.3 0.4 slice_reduce_fusion.2
  107.9 0.4 slice_reduce_fusion.2
  110.4 0.4 slice_reduce_fusion.2
  120.5 0.4 slice_reduce_fusion.2
  123.0 0.4 slice_reduce_fusion.2
  125.5 0.4 slice_reduce_fusion.2
  128.0 0.4 slice_reduce_fusion.2
  135.6 0.4 slice_reduce_fusion.2
  138.1 0.4 slice_reduce_fusion.2
  140.7 0.4 slice_reduce_fusion.2
  143.2 0.4 slice_reduce_fusion.2
  149.0 1.1 gather_fusion.2
  150.5 0.9 copy.66
  151.4 1.6 broadcast_multiply_fusion
  153.0 4.5 %all-to-all-start.2 = ((f32[128,3,4,256]{3,2,1,0:T(4,128)}), f32[128,3,4,256]{3,2,1,0:T(4,128)S(1)}, u32[]{:S(2)}, u32[]{:S(2)}) async-start(f32[128,3,4,256]{3,2,1,0:T(4,128)} %broadcast_multiply_fusion), calls=%async_computation.2 | async-start | bytes 3145728 | tf_op jit(solution)/shard_map/all_to_all | solution.py:34
  158.0 1.1 broadcast_select_fusion.2
  159.2 23.4 %all-to-all-done.2 = f32[128,3,4,256]{3,2,1,0:T(4,128)S(1)} async-done(((f32[128,3,4,256]{3,2,1,0:T(4,128)}), f32[128,3,4,256]{3,2,1,0:T(4,128)S(1)}, u32[]{:S(2)}, u32[]{:S(2)}) %all-to-all-start.2) | async-done | bytes 1572896 | tf_op jit(solution)/shard_map/all_to_all | solution.py:34
  182.6 1.5 copy.73
  184.1 1.9 copy.67
  185.9 1.0 fusion.11
  186.9 0.8 copy.68
  (510 shorter events, 74.2 us)
Async XLA Ops:
  0.6 28.0 %copy-start = (f32[8,8,4,256]{3,2,1,0:T(4,128)S(1)}, f32[8,8,4,256]{3,2,1,0:T(4,128)}, u32[]{:S(2)}) copy-start(f32[8,8,4,256]{3,2,1,0:T(4,128)} %param.10) | copy-start | bytes 786436
  32.6 4.6 %copy-start.3 = (f32[256,4,128]{2,1,0:T(4,128)S(1)}, f32[256,4,128]{2,1,0:T(4,128)}, u32[]{:S(2)}) copy-start(f32[256,4,128]{2,1,0:T(4,128)} %param.11) | copy-start | bytes 1572868
  32.6 29.5 %all-to-all-start.1 = ((f32[128,3,4,256]{3,2,1,0:T(4,128)}), f32[128,3,4,256]{3,2,1,0:T(4,128)S(1)}, u32[]{:S(2)}, u32[]{:S(2)}) async-start(f32[128,3,4,256]{3,2,1,0:T(4,128)} %broadcast_select_fusion), calls=%async_computation.1 | async-start | bytes 3145728 | tf_op jit(solution)/shard_map/all_to_all | solution.py:28
  37.2 3.7 %copy-start.6 = (f32[256,256]{1,0:T(8,128)S(1)}, f32[256,256]{1,0:T(8,128)}, u32[]{:S(2)}) copy-start(f32[256,256]{1,0:T(8,128)} %param.14) | copy-start | bytes 786436
  45.5 18.8 %copy-start.7 = (f32[256,256]{1,0:T(8,128)S(1)}, f32[256,256]{1,0:T(8,128)}, u32[]{:S(2)}) copy-start(f32[256,256]{1,0:T(8,128)} %param.14) | copy-start | bytes 786436
  64.3 3.7 %copy-start.8 = (f32[256,4]{0,1:T(4,128)S(1)}, f32[256,4]{0,1:T(4,128)}, u32[]{:S(2)}) copy-start(f32[256,4]{0,1:T(4,128)} %param.13) | copy-start | bytes 12292
  68.0 0.8 copy-start.1
  69.5 1.0 copy-start.2
  70.6 0.8 copy-start.1
  72.0 1.0 copy-start.2
  73.1 0.8 copy-start.1
  74.6 1.0 copy-start.2
  75.6 0.8 copy-start.1
  77.1 1.0 copy-start.2
  78.1 0.8 copy-start.1
  79.6 1.0 copy-start.2
  80.7 0.8 copy-start.1
  82.1 1.0 copy-start.2
  84.7 1.0 copy-start.2
  87.2 1.0 copy-start.2
  89.7 1.0 copy-start.2
  92.2 1.0 copy-start.2
  94.8 1.0 copy-start.2
  97.3 1.0 copy-start.2
  99.8 1.0 copy-start.2
  102.3 1.0 copy-start.2
  104.9 1.0 copy-start.2
  107.4 1.0 copy-start.2
  109.9 1.0 copy-start.2
  112.4 1.0 copy-start.2
  115.0 1.0 copy-start.2
  117.5 1.0 copy-start.2
  118.5 0.8 copy-start.1
  120.0 1.0 copy-start.2
  122.5 1.0 copy-start.2
  125.1 1.0 copy-start.2
  127.6 1.0 copy-start.2
  130.1 1.0 copy-start.2
  132.6 1.0 copy-start.2
  135.2 1.0 copy-start.2
  137.7 1.0 copy-start.2
  140.2 1.0 copy-start.2
  142.7 1.0 copy-start.2
  145.3 1.0 copy-start.2
  147.8 1.0 copy-start.2
  149.0 2.4 %copy-start.5 = (f32[128,3,256]{2,1,0:T(4,128)S(1)}, f32[128,3,256]{2,1,0:T(4,128)}, u32[]{:S(2)}) copy-start(f32[128,3,256]{2,1,0:T(4,128)} %broadcast_select_fusion.1) | copy-start | bytes 1179652
  153.0 5.0 %copy-start.4 = (f32[256,4,128]{2,1,0:T(4,128)S(1)}, f32[256,4,128]{2,1,0:T(4,128)}, u32[]{:S(2)}) copy-start(f32[256,4,128]{2,1,0:T(4,128)} %param.11) | copy-start | bytes 1572868
  153.0 29.6 %all-to-all-start.2 = ((f32[128,3,4,256]{3,2,1,0:T(4,128)}), f32[128,3,4,256]{3,2,1,0:T(4,128)S(1)}, u32[]{:S(2)}, u32[]{:S(2)}) async-start(f32[128,3,4,256]{3,2,1,0:T(4,128)} %broadcast_multiply_fusion), calls=%async_computation.2 | async-start | bytes 3145728 | tf_op jit(solution)/shard_map/all_to_all | solution.py:34
  (25 other events, 19.7 us)
where the time goes:
time: 190 us; the launch traced here: 188 us
  local copies, waits for them, and re-layouts  86.4 us (45%)
  waiting for transfers between devices  40.1 us (21%)
  other arithmetic  22.8 us (12%)
  blocking collectives  20.8 us (11%)
  starting transfers between devices  9.1 us (5%)
  matrix products  4.46 us (2%)
  loops' own time  2.48 us (1%)
    while x224, local copies, waits for them, and re-layouts  31.4 us
    all_to_all x1, waiting for transfers between devices, route_uptake(): lax.all_to_all(uptake_rows, ('gx', 'gy'), split_axis=0, concat_axis=0, ti...  23.4 us
    all_to_all x1, blocking collectives, route_requests(): lax.all_to_all(wanted, ('gx', 'gy'), split_axis=0, concat_axis=0, tiled=T...  20.8 us
    all_to_all x1, waiting for transfers between devices, route_values(): lax.all_to_all(served, ('gx', 'gy'), split_axis=0, concat_axis=0, tiled=T...  16.6 us
    slice x32, local copies, waits for them, and re-layouts, substep(): return (level + current - incoming, drawn + current[:, :, -1])  12.2 us
    mul x32, local copies, waits for them, and re-layouts, substep(): absorbed = uptake_rate[:, :, None] * level[:, :, :1]  7.06 us
    broadcast_in_dim x32, local copies, waits for them, and re-layouts, substep(): outward = jnp.concatenate([level[:, :, 1:], boundary[:, :, None]], axis=2)  7.01 us
    mul x32, other arithmetic, substep(): current = conductance * (outward - level)  6.77 us
  transfers between devices with their start and end apart: 2, of which 2 were waited for; matrix products, arithmetic and copies ran while one was open for 5% of the time, Pallas kernels for 0%

commit v1 on v0

v1 whole, which is shorter than its diff:
```python
import itertools

import jax
import jax.numpy as jnp
from jax import lax
from jax.experimental import pallas as pl
from jax.experimental.pallas import tpu as pltpu
from jax.sharding import PartitionSpec as P

SUB = 32
CAP = 3
NR = 128
F32 = jnp.float32
BF16 = jnp.bfloat16
MESH = pl.DeviceIdType.MESH
NN = (((1,), (0,)), ((), ()))
NT = (((1,), (1,)), ((), ()))


def hops(o):
    return sum(min(v, 4 - v) for v in o[:3])


OFFSETS = sorted(
    (o for o in itertools.product(range(4), range(4), range(4), range(2)) if any(o)),
    key=lambda o: (-hops(o), o),
)


def coords():
    gx, gy = lax.axis_index("gx"), lax.axis_index("gy")
    return gy // 2, gx // 4, lax.rem(gx, 4), lax.rem(gy, 2)


def partner(here, o):
    x, y, z, c = here
    gx = ((y + o[1]) & 3) * 4 + ((z + o[2]) & 3)
    gy = ((x + o[0]) & 3) * 2 + (c ^ o[3])
    return gx, gy


def dot(a, b, dims=NN):
    return lax.dot_general(a, b, dims, preferred_element_type=F32)


def split2(x):
    high = x.astype(BF16)
    return high, (x - high.astype(F32)).astype(BF16)


def split3(x):
    high, mid = split2(x)
    return high, mid, (x - high.astype(F32) - mid.astype(F32)).astype(BF16)


def row(r):
    return pl.ds(8 * r, 8)


def double_step(level, cond, low, boundary, uptake):
    l0 = level[row(low), :]
    zero = jnp.zeros((8, 128), F32)
    p0 = uptake * l0 if uptake is not None else zero
    p1 = l1 = cp = None
    for r in range(low, NR):
        c = cond[row(r), :]
        outer = level[row(r + 1), :] if r < NR - 1 else boundary
        cur = c * (outer - l0)
        new = l0 + cur - p0 if p0 is not None else l0 + cur
        p0, l0 = cur, outer
        if r == low:
            p1 = uptake * new if uptake is not None else zero
        else:
            cur1 = cp * (new - l1)
            level[row(r - 1), :] = l1 + cur1 - p1
            p1 = cur1
        l1, cp = new, c
    cur1 = cp * (boundary - l1)
    level[row(NR - 1), :] = l1 + cur1 - p1
    return p0 + cur1


def kernel(
    soil_h, rhiz_h, cond_h, upt_h, w_h, tgt_h, tile_h, cnt_s,
    next_o, sink_o,
    soil_v, rhiz_v, cond_v, upt_v, w_v, tgt_v, tile_v, next_v, sink_v,
    pm, cm, tm, um, sel, sb, rb, qb, ret,
    in_sems, out_sems, send_sem, recv_sem, send2_sem, recv2_sem,
):
    here = coords()
    me = lax.axis_index("gx") * 8 + lax.axis_index("gy")
    loads = [
        pltpu.make_async_copy(s, d, in_sems.at[i])
        for i, (s, d) in enumerate(
            [(tgt_h, tgt_v), (tile_h, tile_v), (w_h, w_v), (cond_h, cond_v), (rhiz_h, rhiz_v), (upt_h, upt_v), (soil_h, soil_v)]
        )
    ]
    for c in loads:
        c.start()
    barrier = pltpu.get_barrier_semaphore()
    for o in OFFSETS:
        pl.semaphore_signal(barrier, inc=1, device_id=partner(here, o), device_id_type=MESH)
    count = cnt_s[0]

    for c in loads[:3]:
        c.wait()
    live = lax.broadcasted_iota(jnp.int32, (1, 256), 1) < count
    names = lax.broadcasted_iota(jnp.int32, (128, 256), 0)
    match = jnp.where((names == tgt_v[...]) & live, 1.0, 0.0)
    before = jnp.where(
        lax.broadcasted_iota(jnp.int32, (256, 256), 0) < lax.broadcasted_iota(jnp.int32, (256, 256), 1), 1.0, 0.0
    ).astype(BF16)
    rank = dot(match.astype(BF16), before)
    for k in range(CAP):
        sel[pl.ds(128 * k, 128), :] = jnp.where(rank == k, match, 0.0).astype(BF16)
    w = w_v[...]
    portion = w / jnp.sum(w, axis=1, keepdims=True)
    high, mid = split2(portion)
    for k in range(CAP):
        pick = sel[pl.ds(128 * k, 128), :]
        rows = dot(pick, high) + dot(pick, mid)
        sb[pl.ds(2 * k, 128, stride=8), :] = rows[:, :128]
        sb[pl.ds(2 * k + 1, 128, stride=8), :] = rows[:, 128:]

    for c in loads[3:6]:
        c.wait()
    lives = [lax.broadcasted_iota(jnp.int32, (1, 128), 1) + 128 * half < count for half in range(2)]
    for j in range(8):
        half, f = j // 4, j % 4
        block = pl.ds(512 * half + f, 128, stride=4)
        pm[pl.ds(j, 128, stride=8), :] = rhiz_v[block, :].T
        cm[pl.ds(j, 128, stride=8), :] = jnp.where(lives[half], cond_v[block, :].T, 0.0)
    uptake = jnp.concatenate(
        [jnp.where(lives[half], upt_v[:, pl.ds(128 * half, 128)], 0.0) for half in range(2)], axis=0
    )

    zero, one = jnp.zeros((8, 128), F32), jnp.ones((8, 128), F32)
    for r in range(NR - 32, NR):
        tm[row(r), :] = pm[row(r), :]
        um[row(r), :] = zero
    drawn0, gain = zero, zero
    for g in range(4):
        drawn0 = lax.fori_loop(0, 4, lambda i, d, g=g: d + double_step(tm, cm, NR - 32 + 8 * g, zero, None), drawn0)
        gain = lax.fori_loop(0, 4, lambda i, d, g=g: d + double_step(um, cm, NR - 8 - 8 * g, one, None), gain)

    def as_rows(v):
        return jnp.concatenate([v[0:4], v[4:8]], axis=1)

    tile_row = tile_v[...].astype(F32)
    items = jnp.concatenate(
        [tile_row, jnp.zeros((3, 256), F32), as_rows(drawn0), as_rows(gain), jnp.zeros((4, 256), F32)], axis=0
    )
    meta = jnp.zeros((128, 128), F32)
    for k in range(CAP):
        parts = [jnp.zeros((16 * k, 256), F32)] if k else []
        wide = jnp.concatenate(parts + [items, jnp.zeros((112 - 16 * k, 256), F32)], axis=0)
        pick = sel[pl.ds(128 * k, 128), :]
        for piece in split3(wide):
            meta = meta + dot(pick, piece, NT)
    sb[pl.ds(6, 128, stride=8), :] = meta
    sb[pl.ds(7, 128, stride=8), :] = jnp.zeros((128, 128), F32)

    pl.semaphore_wait(barrier, len(OFFSETS))
    for o in OFFSETS:
        gx, gy = partner(here, o)
        pltpu.make_async_remote_copy(
            sb.at[row(gx * 8 + gy), :], rb.at[row(me), :], send_sem, recv_sem, device_id=(gx, gy), device_id_type=MESH
        ).start()
    rb[row(me), :] = sb[row(me), :]

    lax.fori_loop(0, SUB // 2, lambda i, d: d + double_step(pm, cm, 0, zero, uptake), zero)
    loads[6].wait()
    soil = jnp.concatenate(
        [
            jnp.concatenate([soil_v[pl.ds(4 * half + f, 64, stride=8), :] for half in range(2)], axis=1)
            for f in range(4)
        ],
        axis=0,
    )
    soil_high, soil_mid = split2(soil)

    view = rb.at[pl.ds(0, 8 * 127), :]
    pltpu.make_async_copy(view, view, recv_sem).wait()
    got = jnp.concatenate(
        [
            jnp.concatenate([rb[pl.ds(2 * k + half, 128, stride=8), :] for half in range(2)], axis=1)
            for k in range(CAP)
        ],
        axis=0,
    )
    got_high, got_mid = split2(got)
    field = dot(soil_high, got_high, NT) + dot(soil_high, got_mid, NT) + dot(soil_mid, got_high, NT)
    info = rb[pl.ds(6, 128, stride=8), :].T
    tiles = (lax.broadcasted_iota(jnp.int32, (256, 128), 0) & 63).astype(F32)
    marks, values = [], []
    for k in range(CAP):
        mark = tiles == info[16 * k : 16 * k + 1]
        masked = jnp.where(mark, field[:, 128 * k : 128 * k + 128], 0.0)
        marks.append(mark)
        values.append([jnp.sum(masked[64 * f : 64 * f + 64], axis=0, keepdims=True) for f in range(4)])
    reply = jnp.concatenate(
        [jnp.concatenate(values[k] + [jnp.zeros((4, 128), F32)], axis=0) for k in range(CAP)]
        + [jnp.zeros((128 - 8 * CAP, 128), F32)],
        axis=0,
    )
    qb[:, 0, :] = reply.T
    for o in OFFSETS:
        gx, gy = partner(here, o)
        pltpu.make_async_remote_copy(
            qb.at[gx * 8 + gy], ret.at[me], send2_sem, recv2_sem, device_id=(gx, gy), device_id_type=MESH
        ).start()
    ret[me] = qb[me]

    share = []
    for k in range(CAP):
        drawn = [
            info[16 * k + 4 + f : 16 * k + 5 + f] + info[16 * k + 8 + f : 16 * k + 9 + f] * values[k][f]
            for f in range(4)
        ]
        spread = jnp.concatenate([jnp.broadcast_to(d, (64, 128)) for d in drawn], axis=0)
        share.append(jnp.where(marks[k], spread, 0.0))
    share_high, share_mid = split2(jnp.concatenate(share, axis=1))
    sink = dot(share_high, got_high) + dot(share_high, got_mid) + dot(share_mid, got_high)
    for f in range(4):
        for half in range(2):
            sink_v[pl.ds(4 * half + f, 64, stride=8), :] = sink[64 * f : 64 * f + 64, 128 * half : 128 * half + 128]
    sink_out = pltpu.make_async_copy(sink_v, sink_o, out_sems.at[0])
    sink_out.start()

    view = ret.at[pl.ds(0, 127)]
    pltpu.make_async_copy(view, view, recv2_sem).wait()
    back = ret[:, 0, :].T
    bound = jnp.zeros((8, 256), F32)
    for k in range(CAP):
        pick = sel[pl.ds(128 * k, 128), :]
        for piece in split3(back[8 * k : 8 * k + 8]):
            bound = bound + dot(piece, pick)
    bound = jnp.concatenate([bound[0:4, :128], bound[0:4, 128:]], axis=0)
    for r in range(NR - 32, NR):
        pm[row(r), :] = pm[row(r), :] + bound * um[row(r), :]
    for j in range(8):
        half, f = j // 4, j % 4
        next_v[pl.ds(512 * half + f, 128, stride=4), :] = pm[pl.ds(j, 128, stride=8), :].T
    next_out = pltpu.make_async_copy(next_v, next_o, out_sems.at[1])
    next_out.start()

    view = sb.at[pl.ds(0, 8 * 127), :]
    pltpu.make_async_copy(view, view, send_sem).wait()
    view = qb.at[pl.ds(0, 127)]
    pltpu.make_async_copy(view, view, send2_sem).wait()
    sink_out.wait()
    next_out.wait()


def on_device(
    soil_field, rhizosphere, conductance, uptake_rate, segment_weight, segment_target, segment_tile, segment_count
):
    soil = soil_field.reshape(64, 4, 2, 128).transpose(0, 2, 1, 3).reshape(512, 128)
    vm = pltpu.VMEM
    any_spec = pl.BlockSpec(memory_space=pl.ANY)
    nxt, sink = pl.pallas_call(
        kernel,
        out_shape=(jax.ShapeDtypeStruct((1024, 128), F32), jax.ShapeDtypeStruct((512, 128), F32)),
        in_specs=[any_spec] * 7 + [pl.BlockSpec(memory_space=pltpu.SMEM)],
        out_specs=(any_spec, any_spec),
        scratch_shapes=[
            vm((512, 128), F32), vm((1024, 128), F32), vm((1024, 128), F32), vm((4, 256), F32), vm((256, 256), F32),
            vm((1, 256), jnp.int32), vm((1, 256), jnp.int32), vm((1024, 128), F32), vm((512, 128), F32),
            vm((1024, 128), F32), vm((1024, 128), F32), vm((1024, 128), F32), vm((1024, 128), F32),
            vm((384, 256), BF16), vm((1024, 128), F32), vm((1024, 128), F32),
            vm((128, 1, 128), F32), vm((128, 1, 128), F32),
            pltpu.SemaphoreType.DMA((7,)), pltpu.SemaphoreType.DMA((2,)),
            pltpu.SemaphoreType.DMA(()), pltpu.SemaphoreType.DMA(()),
            pltpu.SemaphoreType.DMA(()), pltpu.SemaphoreType.DMA(()),
        ],
        compiler_params=pltpu.CompilerParams(
            collective_id=0, has_side_effects=True, vmem_limit_bytes=60 * 1024 * 1024
        ),
    )(
        soil,
        rhizosphere.reshape(1024, 128),
        conductance.reshape(1024, 128),
        uptake_rate.T,
        segment_weight,
        segment_target.reshape(1, 256),
        segment_tile.reshape(1, 256),
        segment_count,
    )
    sink = sink.reshape(64, 2, 4, 128).transpose(0, 2, 1, 3)
    return nxt.reshape(256, 4, 128), sink.reshape(8, 8, 4, 256)


def solution(mesh):
    flat = ("gx", "gy")
    return jax.shard_map(
        on_device,
        mesh=mesh,
        in_specs=(
            P("gx", "gy", None, None), P(flat, None, None), P(flat, None, None), P(flat, None), P(flat, None),
            P(flat, None), P(flat), P(flat),
        ),
        out_specs=(P(flat, None, None), P("gx", "gy", None, None)),
        check_vma=False,
    )
```

time: 190 us -> 31.3 us (0.16); the launches traced: 188 us -> 31.2 us
  local copies, waits for them, and re-layouts: 86.4 us -> 2.62 us
  waiting for transfers between devices: 40.1 us -> 0 us
  Pallas kernels: 0 us -> 27.3 us
  other arithmetic: 22.8 us -> 0 us
  blocking collectives: 20.8 us -> 0 us
  starting transfers between devices: 9.1 us -> 0 us
  matrix products: 4.46 us -> 0 us
  loops' own time: 2.48 us -> 0 us
    all_to_all x2 -> x0, waiting for transfers between devices: 40.1 us -> none  [the longest x1 23.4 us: route_uptake(): lax.all_to_all(uptake_rows, ('gx', 'gy'), split_axis=0, concat_axis=0, ti...]
    while x225 -> x0, local copies, waits for them, and re-layouts: 31.7 us -> none
    pallas_call x0 -> x1, Pallas kernels: none -> 27.3 us  [on_device(): pl.pallas_call(kernel, out_shape=(jax.ShapeDtypeStruct((1024, 128), F32),...]
    all_to_all x1 -> x0, blocking collectives: 20.8 us -> none  [route_requests(): lax.all_to_all(wanted, ('gx', 'gy'), split_axis=0, concat_axis=0, tiled=T...]
    slice x64 -> x0, local copies, waits for them, and re-layouts: 18.8 us -> none  [the longest x32 12.2 us: substep(): return (level + current - incoming, drawn + current[:, :, -1])]
    gather x7 -> x0, local copies, waits for them, and re-layouts: 9.44 us -> none  [the longest x2 3.35 us: on_device(): slot_portion = jnp.take(portion, slot_index, axis=0)]
    all_to_all x2 -> x0, starting transfers between devices: 9.1 us -> none  [the longest x1 4.61 us: route_values(): lax.all_to_all(served, ('gx', 'gy'), split_axis=0, concat_axis=0, tiled=T...]
    mul x65 -> x0, other arithmetic: 8.55 us -> none  [the longest x32 6.77 us: substep(): current = conductance * (outward - level)]
  transfers between devices with their start and end apart: 2 -> 0, of which waited for: 2 -> 0; matrix products, arithmetic and copies ran while one was open for 5% -> 0% of each run, Pallas kernels for 0% -> 0%
where the time goes in v1:
time: 31.3 us; the launch traced here: 31.2 us
  Pallas kernels  27.3 us (87%)
  local copies, waits for them, and re-layouts  2.62 us (8%)
  between operations  1.3 us (4%)
    pallas_call x1, Pallas kernels, on_device(): pl.pallas_call(kernel, out_shape=(jax.ShapeDtypeStruct((1024, 128), F32),...  27.3 us
    unnamed x4, local copies, waits for them, and re-layouts  2.62 us

profile of v1, /device:TPU:1, one launch (start us, length us, event | category | flops | bytes accessed | tf_op | source)
XLA Modules:
  0.0 31.2 jit_solution(18042856214232594718)
XLA Ops:
  1.3 27.3 %shard_map.95 = (f32[1024,128]{1,0:T(8,128)}, f32[512,128]{1,0:T(8,128)}) custom-call(f32[512,128]{1,0:T(8,128)} %bitcast.20, f32[1024,128]{1,0:T(8,128)} %bitcast.16, f32[1024,128]{1,0:T(8,128)} %bitcast.17, f32[4,256]{1,0:T(4,128)} %bitcast.21, f32[256,256]{1,0:T(8,128)} %w_h.1, s32[1,256]{1,0:T(1,128)} %bitcast.22, s32[1,256]{1,0:T(1,128)} %bitcast.23, ...), custom_call_target="tpu_custom_call" | custom-call | tf_op jit(solution)/shard_map/pallas_call | solution.py:261
  28.5 0.0 copy-start
  28.6 1.9 %copy.15 = f32[256,4,128]{2,1,0:T(4,128)} copy(f32[256,4,128]{2,1,0:T(4,128)} %bitcast.18) | data formatting | bytes 1048576
  30.5 0.0 copy-done
  30.5 0.7 %copy.16 = f32[8,8,4,256]{3,2,1,0:T(4,128)} copy(f32[8,8,4,256]{3,2,1,0:T(4,128)S(1)} %bitcast.19) | data formatting | bytes 524288
Async XLA Ops:
  28.5 1.9 %copy-start = (f32[512,128]{1,0:T(8,128)S(1)}, f32[512,128]{1,0:T(8,128)}, u32[]{:S(2)}) copy-start(f32[512,128]{1,0:T(8,128)} %get-tuple-element.5) | copy-start | bytes 786436

commit v2 on v1

v2 whole, which is shorter than its diff:
```python
import itertools

import jax
import jax.numpy as jnp
from jax import lax
from jax.experimental import pallas as pl
from jax.experimental.pallas import tpu as pltpu
from jax.sharding import PartitionSpec as P

SUB = 32
CAP = 3
NR = 128
F32 = jnp.float32
BF16 = jnp.bfloat16
MESH = pl.DeviceIdType.MESH
NN = (((1,), (0,)), ((), ()))
NT = (((1,), (1,)), ((), ()))


MESSAGE = 7


def hops(o):
    return sum(min(v, 4 - v) for v in o[:2])


PLANE = sorted((o for o in itertools.product(range(4), range(4), range(2)) if any(o)), key=lambda o: (-hops(o), o))


def coords():
    gx, gy = lax.axis_index("gx"), lax.axis_index("gy")
    return gy // 2, gx // 4, lax.rem(gx, 4), lax.rem(gy, 2)


def device(x, y, z, c):
    return y * 4 + z, x * 2 + c


def place(x, y, z, c):
    return z * 32 + y * 8 + x * 2 + c


def dot(a, b, dims=NN):
    return lax.dot_general(a, b, dims, preferred_element_type=F32)


def split2(x):
    high = x.astype(BF16)
    return high, (x - high.astype(F32)).astype(BF16)


def split3(x):
    high, mid = split2(x)
    return high, mid, (x - high.astype(F32) - mid.astype(F32)).astype(BF16)


def row(r):
    return pl.ds(8 * r, 8)


def double_step(level, cond, low, boundary, uptake):
    l0 = level[row(low), :]
    zero = jnp.zeros((8, 128), F32)
    p0 = uptake * l0 if uptake is not None else zero
    p1 = l1 = cp = None
    for r in range(low, NR):
        c = cond[row(r), :]
        outer = level[row(r + 1), :] if r < NR - 1 else boundary
        cur = c * (outer - l0)
        new = l0 + cur - p0 if p0 is not None else l0 + cur
        p0, l0 = cur, outer
        if r == low:
            p1 = uptake * new if uptake is not None else zero
        else:
            cur1 = cp * (new - l1)
            level[row(r - 1), :] = l1 + cur1 - p1
            p1 = cur1
        l1, cp = new, c
    cur1 = cp * (boundary - l1)
    level[row(NR - 1), :] = l1 + cur1 - p1
    return p0 + cur1


def exchange(
    soil_h, rhiz_h, cond_h, upt_h, w_h, tgt_h, tile_h, cnt_s,
    pm_o, um_o, sel_o, sink_o, ret,
    soil_v, rhiz_v, cond_v, upt_v, w_v, tgt_v, tile_v, sink_v,
    pm, cm, tm, um, sel, sb, rb, qb, info_v,
    in_sems, out_sems, plane_sem, send_sem, recv_sem, send2_sem, recv2_sem,
):
    x, y, z, c = coords()
    me = place(x, y, z, c)
    loads = [
        pltpu.make_async_copy(s, d, in_sems.at[i])
        for i, (s, d) in enumerate(
            [(tgt_h, tgt_v), (tile_h, tile_v), (w_h, w_v), (cond_h, cond_v), (rhiz_h, rhiz_v), (upt_h, upt_v), (soil_h, soil_v)]
        )
    ]
    for load in loads:
        load.start()

    def beside(o):
        return (x + o[0]) & 3, (y + o[1]) & 3, c ^ o[2]

    barrier = pltpu.get_barrier_semaphore()
    for dz in (2, 1, 3):
        pl.semaphore_signal(barrier, inc=1, device_id=device(x, y, (z + dz) & 3, c), device_id_type=MESH)
    for o in PLANE:
        ox, oy, oc = beside(o)
        pl.semaphore_signal(barrier, inc=1, device_id=device(ox, oy, z, oc), device_id_type=MESH)
    count = cnt_s[0]

    def send(p, src, dst, send_s, recv_s, rows):
        def copy_to(x, y, c):
            there = place(x, y, p, c)
            return pltpu.make_async_remote_copy(
                src.at[rows(there)], dst.at[rows(me)], send_s, recv_s.at[z],
                device_id=device(x, y, p, c), device_id_type=MESH,
            )

        for o in PLANE:
            copy_to(*beside(o)).start()

        @pl.when(z != p)
        def _():
            copy_to(x, y, c).start()

        @pl.when(z == p)
        def _():
            pltpu.make_async_copy(src.at[rows(me)], dst.at[rows(me)], recv_s.at[z]).start()

    def block(r):
        return pl.ds(8 * r, MESSAGE)

    for load in loads[:3]:
        load.wait()
    live = lax.broadcasted_iota(jnp.int32, (1, 256), 1) < count
    names = lax.broadcasted_iota(jnp.int32, (128, 256), 0)
    target = tgt_v[...]
    target = ((target >> 3) & 3) * 32 + (target >> 5) * 8 + (target & 7)
    match = jnp.where((names == target) & live, 1.0, 0.0)
    before = jnp.where(
        lax.broadcasted_iota(jnp.int32, (256, 256), 0) < lax.broadcasted_iota(jnp.int32, (256, 256), 1), 1.0, 0.0
    ).astype(BF16)
    rank = dot(match.astype(BF16), before)
    for k in range(CAP):
        sel[pl.ds(128 * k, 128), :] = jnp.where(rank == k, match, 0.0).astype(BF16)
    w = w_v[...]
    portion = w / jnp.sum(w, axis=1, keepdims=True)
    high, mid = split2(portion)
    for k in range(CAP):
        pick = sel[pl.ds(128 * k, 128), :]
        rows = dot(pick, high) + dot(pick, mid)
        sb[pl.ds(2 * k, 128, stride=8), :] = rows[:, :128]
        sb[pl.ds(2 * k + 1, 128, stride=8), :] = rows[:, 128:]

    for load in loads[3:6]:
        load.wait()
    lives = [lax.broadcasted_iota(jnp.int32, (1, 128), 1) + 128 * half < count for half in range(2)]
    for j in range(8):
        half, f = j // 4, j % 4
        rows = pl.ds(512 * half + f, 128, stride=4)
        pm[pl.ds(j, 128, stride=8), :] = rhiz_v[rows, :].T
        cm[pl.ds(j, 128, stride=8), :] = jnp.where(lives[half], cond_v[rows, :].T, 0.0)
    uptake = jnp.concatenate(
        [jnp.where(lives[half], upt_v[:, pl.ds(128 * half, 128)], 0.0) for half in range(2)], axis=0
    )

    zero, one = jnp.zeros((8, 128), F32), jnp.ones((8, 128), F32)
    for r in range(NR - 32, NR):
        tm[row(r), :] = pm[row(r), :]
        um[row(r), :] = zero
    drawn0, gain = zero, zero
    for g in range(4):
        drawn0 = lax.fori_loop(0, 4, lambda i, d, g=g: d + double_step(tm, cm, NR - 32 + 8 * g, zero, None), drawn0)
        gain = lax.fori_loop(0, 4, lambda i, d, g=g: d + double_step(um, cm, NR - 8 - 8 * g, one, None), gain)

    def as_rows(v):
        return jnp.concatenate([v[0:4], v[4:8]], axis=1)

    tile_row = tile_v[...].astype(F32)
    items = jnp.concatenate(
        [tile_row, jnp.zeros((3, 256), F32), as_rows(drawn0), as_rows(gain), jnp.zeros((4, 256), F32)], axis=0
    )
    meta = jnp.zeros((128, 128), F32)
    for k in range(CAP):
        parts = [jnp.zeros((32 * k, 256), F32)] if k else []
        wide = jnp.concatenate(parts + [items, jnp.zeros((112 - 32 * k, 256), F32)], axis=0)
        pick = sel[pl.ds(128 * k, 128), :]
        for piece in split3(wide):
            meta = meta + dot(pick, piece, NT)
    sb[pl.ds(6, 128, stride=8), :] = meta


    loads[6].wait()
    soil = jnp.concatenate(
        [
            jnp.concatenate([soil_v[pl.ds(4 * half + f, 64, stride=8), :] for half in range(2)], axis=1)
            for f in range(4)
        ],
        axis=0,
    )
    soil_high, soil_mid = split2(soil)
    tiles = (lax.broadcasted_iota(jnp.int32, (256, 128), 0) & 63).astype(F32)

    def arrived(p):
        blank = [jnp.zeros((32, 128), F32)]
        halves = [[rb[pl.ds(256 * p + 2 * k + half, 32, stride=8), :] for k in range(CAP)] for half in range(2)]
        return split2(jnp.concatenate([jnp.concatenate(half + blank, axis=0) for half in halves], axis=1))

    @pl.when(z < 0)
    def _():
        lax.fori_loop(0, SUB // 2, lambda i, d: d + double_step(pm, cm, 0, zero, uptake), zero)

    pl.semaphore_wait(barrier, len(PLANE) + 3)
    for dz in (2, 1, 3):
        pl.semaphore_signal(plane_sem.at[z], inc=1, device_id=device(x, y, (z + dz) & 3, c), device_id_type=MESH)

    def give(p):
        @pl.when(z != p)
        def _():
            pl.semaphore_wait(plane_sem.at[p], 1)

        send(p, sb, rb, send_sem, recv_sem, block)

    def answer(p):
        view = rb.at[pl.ds(0, 32 * MESSAGE), :]
        pltpu.make_async_copy(view, view, recv_sem.at[p]).wait()
        high, mid = arrived(p)
        field = dot(soil_high, high, NT) + dot(soil_high, mid, NT) + dot(soil_mid, high, NT)
        items = rb[pl.ds(256 * p + 6, 32, stride=8), :]
        info = jnp.concatenate(
            [items, pltpu.roll(items, 96, 1), pltpu.roll(items, 64, 1), jnp.full((32, 128), -1.0, F32)], axis=0
        ).T
        masked = jnp.where(tiles == info[0:1], field, 0.0)
        values = [jnp.sum(masked[64 * f : 64 * f + 64], axis=0, keepdims=True) for f in range(4)]
        reply = jnp.concatenate(values + [jnp.zeros((124, 128), F32)], axis=0).T
        qb[pl.ds(32 * p, 32), 0, :] = reply[0:32] + pltpu.roll(reply[32:64], 8, 1) + pltpu.roll(reply[64:96], 16, 1)
        send(p, qb, ret, send2_sem, recv2_sem, lambda r: r)
        info_v[pl.ds(24 * p, 24), :] = jnp.concatenate([info[0:12]] + values + [jnp.zeros((8, 128), F32)], axis=0)

    @pl.when(z == 9)
    def _():
        for p in range(4):
            give(p)
            answer(p)

    @pl.when(jnp.logical_not(z == 9))
    def _():
        for p in (0, 1, 2, 3):
            give(p)
        for p in range(4):
            answer(p)

    sink = jnp.zeros((256, 256), F32)
    for p in range(4):
        info = info_v[pl.ds(24 * p, 24), :]
        drawn = info[4:8] + info[8:12] * info[12:16]
        spread = jnp.concatenate([jnp.broadcast_to(drawn[f : f + 1], (64, 128)) for f in range(4)], axis=0)
        share_high, share_mid = split2(jnp.where(tiles == info[0:1], spread, 0.0))
        high, mid = arrived(p)
        sink = sink + dot(share_high, high) + dot(share_high, mid) + dot(share_mid, high)
    for f in range(4):
        for half in range(2):
            sink_v[pl.ds(4 * half + f, 64, stride=8), :] = sink[64 * f : 64 * f + 64, 128 * half : 128 * half + 128]
    outs = [
        pltpu.make_async_copy(s, d, out_sems.at[i])
        for i, (s, d) in enumerate([(sink_v, sink_o), (pm, pm_o), (um.at[pl.ds(8 * (NR - 32), 256), :], um_o), (sel, sel_o)])
    ]
    outs[0].start()
    outs[2].start()
    outs[3].start()
    lax.fori_loop(0, 16, lambda i, d: d + double_step(pm, cm, 0, zero, uptake), zero)
    outs[1].start()

    for p in range(4):
        view = ret.at[pl.ds(0, 32)]
        pltpu.make_async_copy(view, view, recv2_sem.at[p]).wait()
    view = sb.at[pl.ds(0, 127 * MESSAGE), :]
    pltpu.make_async_copy(view, view, send_sem).wait()
    view = qb.at[pl.ds(0, 127)]
    pltpu.make_async_copy(view, view, send2_sem).wait()
    for out in outs:
        out.wait()


def finish(pm_h, um_h, sel_h, sink_h, ret_h, next_o, sink_o, pm, um, sel, ret, next_v, sink_v, in_sems, out_sems):
    sink_copy = pltpu.make_async_copy(sink_v, sink_o, out_sems.at[2])
    loads = [
        pltpu.make_async_copy(s, d, in_sems.at[i])
        for i, (s, d) in enumerate([(ret_h, ret), (sel_h, sel), (um_h, um), (pm_h, pm), (sink_h, sink_v)])
    ]
    for load in loads:
        load.start()
    loads[0].wait()
    loads[1].wait()
    back = ret[...].T
    bound = jnp.zeros((8, 256), F32)
    for k in range(CAP):
        pick = sel[pl.ds(128 * k, 128), :]
        for piece in split3(back[8 * k : 8 * k + 8]):
            bound = bound + dot(piece, pick)
    bound = jnp.concatenate([bound[0:4, :128], bound[0:4, 128:]], axis=0)
    loads[4].wait()
    sink_copy.start()
    loads[2].wait()
    loads[3].wait()
    for r in range(32):
        at = row(NR - 32 + r)
        pm[at, :] = pm[at, :] + bound * um[row(r), :]
    for half in range(2):
        for f in range(4):
            next_v[pl.ds(512 * half + f, 128, stride=4), :] = pm[pl.ds(4 * half + f, 128, stride=8), :].T
        rows = pl.ds(512 * half, 512)
        pltpu.make_async_copy(next_v.at[rows, :], next_o.at[rows, :], out_sems.at[half]).start()
    for half in range(2):
        rows = pl.ds(512 * half, 512)
        pltpu.make_async_copy(next_v.at[rows, :], next_o.at[rows, :], out_sems.at[half]).wait()
    sink_copy.wait()


def on_device(
    soil_field, rhizosphere, conductance, uptake_rate, segment_weight, segment_target, segment_tile, segment_count
):
    soil = soil_field.reshape(64, 4, 2, 128).transpose(0, 2, 1, 3).reshape(512, 128)
    vm, dma = pltpu.VMEM, pltpu.SemaphoreType.DMA
    any_spec = pl.BlockSpec(memory_space=pl.ANY)
    pm, um, sel, sink, ret = pl.pallas_call(
        exchange,
        out_shape=(
            jax.ShapeDtypeStruct((1024, 128), F32), jax.ShapeDtypeStruct((256, 128), F32),
            jax.ShapeDtypeStruct((384, 256), BF16), jax.ShapeDtypeStruct((512, 128), F32),
            jax.ShapeDtypeStruct((128, 1, 128), F32),
        ),
        in_specs=[any_spec] * 7 + [pl.BlockSpec(memory_space=pltpu.SMEM)],
        out_specs=(any_spec,) * 5,
        scratch_shapes=[
            vm((512, 128), F32), vm((1024, 128), F32), vm((1024, 128), F32), vm((4, 256), F32), vm((256, 256), F32),
            vm((1, 256), jnp.int32), vm((1, 256), jnp.int32), vm((512, 128), F32),
            vm((1024, 128), F32), vm((1024, 128), F32), vm((1024, 128), F32), vm((1024, 128), F32),
            vm((384, 256), BF16), vm((1024, 128), F32), vm((1024, 128), F32), vm((128, 1, 128), F32), vm((96, 128), F32),
            dma((7,)), dma((4,)), pltpu.SemaphoreType.REGULAR((4,)), dma(()), dma((4,)), dma(()), dma((4,)),
        ],
        compiler_params=pltpu.CompilerParams(
            collective_id=0, has_side_effects=True, vmem_limit_bytes=60 * 1024 * 1024
        ),
    )(
        soil,
        rhizosphere.reshape(1024, 128),
        conductance.reshape(1024, 128),
        uptake_rate.T,
        segment_weight,
        segment_target.reshape(1, 256),
        segment_tile.reshape(1, 256),
        segment_count,
    )
    nxt, sink = pl.pallas_call(
        finish,
        out_shape=(jax.ShapeDtypeStruct((1024, 128), F32), jax.ShapeDtypeStruct((512, 128), F32)),
        in_specs=[any_spec] * 5,
        out_specs=(any_spec,) * 2,
        scratch_shapes=[
            vm((1024, 128), F32), vm((256, 128), F32), vm((384, 256), BF16), vm((128, 128), F32), vm((1024, 128), F32), vm((512, 128), F32),
            dma((5,)), dma((3,)),
        ],
        compiler_params=pltpu.CompilerParams(vmem_limit_bytes=60 * 1024 * 1024),
    )(pm, um, sel, sink, ret.reshape(128, 128))
    sink = sink.reshape(64, 2, 4, 128).transpose(0, 2, 1, 3)
    return nxt.reshape(256, 4, 128), sink.reshape(8, 8, 4, 256)


def solution(mesh):
    flat = ("gx", "gy")
    return jax.shard_map(
        on_device,
        mesh=mesh,
        in_specs=(
            P("gx", "gy", None, None), P(flat, None, None), P(flat, None, None), P(flat, None), P(flat, None),
            P(flat, None), P(flat), P(flat),
        ),
        out_specs=(P(flat, None, None), P("gx", "gy", None, None)),
        check_vma=False,
    )
```

time: 31.3 us -> 28.3 us (0.904)
  local copies, waits for them, and re-layouts: 2.62 us -> 0 us
  Pallas kernels: 27.3 us -> 26.9 us
    unnamed x4 -> x0, local copies, waits for them, and re-layouts: 2.62 us -> none
    pallas_call x1 -> x2, Pallas kernels: 27.3 us -> 26.9 us  [the longest x1 24.6 us: on_device(): pl.pallas_call(exchange, out_shape=(jax.ShapeDtypeStruct((1024, 128), F32...]
where the time goes in v2:
time: 28.3 us; the launch traced here: 28.2 us
  Pallas kernels  26.9 us (95%)
  between operations  1.29 us (5%)
    pallas_call x1, Pallas kernels, on_device(): pl.pallas_call(exchange, out_shape=(jax.ShapeDtypeStruct((1024, 128), F32...  24.6 us
    pallas_call x1, Pallas kernels, on_device(): pl.pallas_call(finish, out_shape=(jax.ShapeDtypeStruct((1024, 128), F32),...  2.31 us

profile of v2, /device:TPU:1, one launch (start us, length us, event | category | flops | bytes accessed | tf_op | source)
XLA Modules:
  0.0 28.2 jit_solution(2672728104562442274)
XLA Ops:
  1.3 24.6 %shard_map.95 = (f32[1024,128]{1,0:T(8,128)}, f32[256,128]{1,0:T(8,128)}, bf16[384,256]{1,0:T(8,128)(2,1)}, f32[512,128]{1,0:T(8,128)}, f32[128,1,128]{2,1,0:T(1,128)}) custom-call(f32[512,128]{1,0:T(8,128)} %bitcast.19, f32[1024,128]{1,0:T(8,128)} %bitcast.17, f32[1024,128]{1,0:T(8,128)} %bitcast.18, f32[4,256]{1,0:T(4,128)} %bitcast.21, f32[256,256]{1,0:T(8,128)} %w_h.1, ...), custom_call_target="tpu_custom_call" | custom-call | tf_op jit(solution)/shard_map/pallas_call | solution.py:328
  25.8 2.3 %shard_map.96 = (f32[1024,128]{1,0:T(8,128)}, f32[512,128]{1,0:T(8,128)}) custom-call(f32[1024,128]{1,0:T(8,128)} %get-tuple-element.9.pm_h, f32[256,128]{1,0:T(8,128)} %get-tuple-element.10.um_h, bf16[384,256]{1,0:T(8,128)(2,1)} %get-tuple-element.11.sel_h, f32[512,128]{1,0:T(8,128)} %get-tuple-element.12.sink_h, f32[128,128]{1,0:T(8,128)} %bitcast.20), custom_call_target="tpu_custom_call" | custom-call | tf_op jit(solution)/shard_map/pallas_call | solution.py:357

commit v3 on v2

--- a/solution.py
+++ b/solution.py
@@ -83,10 +83,10 @@
 
 def exchange(
     soil_h, rhiz_h, cond_h, upt_h, w_h, tgt_h, tile_h, cnt_s,
-    pm_o, um_o, sel_o, sink_o, ret,
-    soil_v, rhiz_v, cond_v, upt_v, w_v, tgt_v, tile_v, sink_v,
-    pm, cm, tm, um, sel, sb, rb, qb, info_v,
-    in_sems, out_sems, plane_sem, send_sem, recv_sem, send2_sem, recv2_sem,
+    pm, um, sel, sink_v, ret,
+    soil_v, rhiz_v, cond_v, upt_v, w_v, tgt_v, tile_v,
+    cm, tm, sb, rb, qb, info_v,
+    in_sems, plane_sem, send_sem, recv_sem, send2_sem, recv2_sem,
 ):
     x, y, z, c = coords()
     me = place(x, y, z, c)
@@ -96,8 +96,6 @@
             [(tgt_h, tgt_v), (tile_h, tile_v), (w_h, w_v), (cond_h, cond_v), (rhiz_h, rhiz_v), (upt_h, upt_v), (soil_h, soil_v)]
         )
     ]
-    for load in loads:
-        load.start()
 
     def beside(o):
         return (x + o[0]) & 3, (y + o[1]) & 3, c ^ o[2]
@@ -108,6 +106,8 @@
     for o in PLANE:
         ox, oy, oc = beside(o)
         pl.semaphore_signal(barrier, inc=1, device_id=device(ox, oy, z, oc), device_id_type=MESH)
+    for load in loads:
+        load.start()
     count = cnt_s[0]
 
     def send(p, src, dst, send_s, recv_s, rows):
@@ -166,6 +166,14 @@
         [jnp.where(lives[half], upt_v[:, pl.ds(128 * half, 128)], 0.0) for half in range(2)], axis=0
     )
 
+    def tell():
+        pl.semaphore_wait(barrier, len(PLANE) + 3)
+        for dz in (2, 1, 3):
+            pl.semaphore_signal(plane_sem.at[z], inc=1, device_id=device(x, y, (z + dz) & 3, c), device_id_type=MESH)
+
+    late = (x >= 2) & (y >= 2) & (z >= 2)
+    pl.when(late)(tell)
+
     zero, one = jnp.zeros((8, 128), F32), jnp.ones((8, 128), F32)
     for r in range(NR - 32, NR):
         tm[row(r), :] = pm[row(r), :]
@@ -208,13 +216,7 @@
         halves = [[rb[pl.ds(256 * p + 2 * k + half, 32, stride=8), :] for k in range(CAP)] for half in range(2)]
         return split2(jnp.concatenate([jnp.concatenate(half + blank, axis=0) for half in halves], axis=1))
 
-    @pl.when(z < 0)
-    def _():
-        lax.fori_loop(0, SUB // 2, lambda i, d: d + double_step(pm, cm, 0, zero, uptake), zero)
-
-    pl.semaphore_wait(barrier, len(PLANE) + 3)
-    for dz in (2, 1, 3):
-        pl.semaphore_signal(plane_sem.at[z], inc=1, device_id=device(x, y, (z + dz) & 3, c), device_id_type=MESH)
+    pl.when(jnp.logical_not(late))(tell)
 
     def give(p):
         @pl.when(z != p)
@@ -239,18 +241,10 @@
         send(p, qb, ret, send2_sem, recv2_sem, lambda r: r)
         info_v[pl.ds(24 * p, 24), :] = jnp.concatenate([info[0:12]] + values + [jnp.zeros((8, 128), F32)], axis=0)
 
-    @pl.when(z == 9)
-    def _():
-        for p in range(4):
-            give(p)
-            answer(p)
-
-    @pl.when(jnp.logical_not(z == 9))
-    def _():
-        for p in (0, 1, 2, 3):
-            give(p)
-        for p in range(4):
-            answer(p)
+    for p in range(4):
+        give(p)
+    for p in range(4):
+        answer(p)
 
     sink = jnp.zeros((256, 256), F32)
     for p in range(4):
@@ -263,15 +257,7 @@
     for f in range(4):
         for half in range(2):
             sink_v[pl.ds(4 * half + f, 64, stride=8), :] = sink[64 * f : 64 * f + 64, 128 * half : 128 * half + 128]
-    outs = [
-        pltpu.make_async_copy(s, d, out_sems.at[i])
-        for i, (s, d) in enumerate([(sink_v, sink_o), (pm, pm_o), (um.at[pl.ds(8 * (NR - 32), 256), :], um_o), (sel, sel_o)])
-    ]
-    outs[0].start()
-    outs[2].start()
-    outs[3].start()
-    lax.fori_loop(0, 16, lambda i, d: d + double_step(pm, cm, 0, zero, uptake), zero)
-    outs[1].start()
+    lax.fori_loop(0, SUB // 2, lambda i, d: d + double_step(pm, cm, 0, zero, uptake), zero)
 
     for p in range(4):
         view = ret.at[pl.ds(0, 32)]
@@ -280,37 +266,26 @@
     pltpu.make_async_copy(view, view, send_sem).wait()
     view = qb.at[pl.ds(0, 127)]
     pltpu.make_async_copy(view, view, send2_sem).wait()
-    for out in outs:
-        out.wait()
-
-
-def finish(pm_h, um_h, sel_h, sink_h, ret_h, next_o, sink_o, pm, um, sel, ret, next_v, sink_v, in_sems, out_sems):
-    sink_copy = pltpu.make_async_copy(sink_v, sink_o, out_sems.at[2])
-    loads = [
-        pltpu.make_async_copy(s, d, in_sems.at[i])
-        for i, (s, d) in enumerate([(ret_h, ret), (sel_h, sel), (um_h, um), (pm_h, pm), (sink_h, sink_v)])
-    ]
-    for load in loads:
-        load.start()
-    loads[0].wait()
-    loads[1].wait()
-    back = ret[...].T
+
+
+def finish(pm, um, sel, sink, ret, next_o, sink_o, last, next_v, out_sems):
+    sink_copy = pltpu.make_async_copy(sink, sink_o, out_sems.at[2])
+    sink_copy.start()
+    back = jnp.concatenate(split2(ret[:, 0, :].T[0:32]), axis=0)
     bound = jnp.zeros((8, 256), F32)
     for k in range(CAP):
-        pick = sel[pl.ds(128 * k, 128), :]
-        for piece in split3(back[8 * k : 8 * k + 8]):
-            bound = bound + dot(piece, pick)
+        part = dot(back, sel[pl.ds(128 * k, 128), :])
+        bound = bound + part[8 * k : 8 * k + 8] + part[32 + 8 * k : 40 + 8 * k]
     bound = jnp.concatenate([bound[0:4, :128], bound[0:4, 128:]], axis=0)
-    loads[4].wait()
-    sink_copy.start()
-    loads[2].wait()
-    loads[3].wait()
-    for r in range(32):
-        at = row(NR - 32 + r)
-        pm[at, :] = pm[at, :] + bound * um[row(r), :]
+    for r in range(NR - 32, NR):
+        last[row(r - NR + 32), :] = pm[row(r), :] + bound * um[row(r), :]
     for half in range(2):
         for f in range(4):
-            next_v[pl.ds(512 * half + f, 128, stride=4), :] = pm[pl.ds(4 * half + f, 128, stride=8), :].T
+            j = 4 * half + f
+            block = jnp.concatenate(
+                [pm[pl.ds(j, NR - 32, stride=8), :], last[pl.ds(j, 32, stride=8), :]], axis=0
+            )
+            next_v[pl.ds(512 * half + f, 128, stride=4), :] = block.T
         rows = pl.ds(512 * half, 512)
         pltpu.make_async_copy(next_v.at[rows, :], next_o.at[rows, :], out_sems.at[half]).start()
     for half in range(2):
@@ -324,47 +299,45 @@
 ):
     soil = soil_field.reshape(64, 4, 2, 128).transpose(0, 2, 1, 3).reshape(512, 128)
     vm, dma = pltpu.VMEM, pltpu.SemaphoreType.DMA
-    any_spec = pl.BlockSpec(memory_space=pl.ANY)
+    any_spec, vmem_spec = pl.BlockSpec(memory_space=pl.ANY), pl.BlockSpec(memory_space=pltpu.VMEM)
+
+    def hbm(a):
+        return pltpu.with_memory_space_constraint(a, pltpu.HBM)
+
     pm, um, sel, sink, ret = pl.pallas_call(
         exchange,
         out_shape=(
-            jax.ShapeDtypeStruct((1024, 128), F32), jax.ShapeDtypeStruct((256, 128), F32),
-            jax.ShapeDtypeStruct((384, 256), BF16), jax.ShapeDtypeStruct((512, 128), F32),
-            jax.ShapeDtypeStruct((128, 1, 128), F32),
+            vm((1024, 128), F32), vm((1024, 128), F32), vm((384, 256), BF16), vm((512, 128), F32), vm((128, 1, 128), F32),
         ),
         in_specs=[any_spec] * 7 + [pl.BlockSpec(memory_space=pltpu.SMEM)],
-        out_specs=(any_spec,) * 5,
+        out_specs=(vmem_spec,) * 5,
         scratch_shapes=[
             vm((512, 128), F32), vm((1024, 128), F32), vm((1024, 128), F32), vm((4, 256), F32), vm((256, 256), F32),
-            vm((1, 256), jnp.int32), vm((1, 256), jnp.int32), vm((512, 128), F32),
-            vm((1024, 128), F32), vm((1024, 128), F32), vm((1024, 128), F32), vm((1024, 128), F32),
-            vm((384, 256), BF16), vm((1024, 128), F32), vm((1024, 128), F32), vm((128, 1, 128), F32), vm((96, 128), F32),
-            dma((7,)), dma((4,)), pltpu.SemaphoreType.REGULAR((4,)), dma(()), dma((4,)), dma(()), dma((4,)),
+            vm((1, 256), jnp.int32), vm((1, 256), jnp.int32), vm((1024, 128), F32), vm((1024, 128), F32),
+            vm((1024, 128), F32), vm((1024, 128), F32), vm((128, 1, 128), F32), vm((96, 128), F32),
+            dma((7,)), pltpu.SemaphoreType.REGULAR((4,)), dma(()), dma((4,)), dma(()), dma((4,)),
         ],
         compiler_params=pltpu.CompilerParams(
-            collective_id=0, has_side_effects=True, vmem_limit_bytes=60 * 1024 * 1024
+            collective_id=0, has_side_effects=True, vmem_limit_bytes=32 * 1024 * 1024
         ),
     )(
-        soil,
-        rhizosphere.reshape(1024, 128),
-        conductance.reshape(1024, 128),
-        uptake_rate.T,
-        segment_weight,
-        segment_target.reshape(1, 256),
-        segment_tile.reshape(1, 256),
+        hbm(soil),
+        hbm(rhizosphere.reshape(1024, 128)),
+        hbm(conductance.reshape(1024, 128)),
+        hbm(uptake_rate.T),
+        hbm(segment_weight),
+        hbm(segment_target.reshape(1, 256)),
+        hbm(segment_tile.reshape(1, 256)),
         segment_count,
     )
     nxt, sink = pl.pallas_call(
         finish,
         out_shape=(jax.ShapeDtypeStruct((1024, 128), F32), jax.ShapeDtypeStruct((512, 128), F32)),
-        in_specs=[any_spec] * 5,
+        in_specs=[vmem_spec] * 5,
         out_specs=(any_spec,) * 2,
-        scratch_shapes=[
-            vm((1024, 128), F32), vm((256, 128), F32), vm((384, 256), BF16), vm((128, 128), F32), vm((1024, 128), F32), vm((512, 128), F32),
-            dma((5,)), dma((3,)),
-        ],
-        compiler_params=pltpu.CompilerParams(vmem_limit_bytes=60 * 1024 * 1024),
-    )(pm, um, sel, sink, ret.reshape(128, 128))
+        scratch_shapes=[vm((256, 128), F32), vm((1024, 128), F32), dma((3,))],
+        compiler_params=pltpu.CompilerParams(vmem_limit_bytes=16 * 1024 * 1024),
+    )(*(pltpu.with_memory_space_constraint(a, pltpu.VMEM) for a in (pm, um, sel, sink, ret)))
     sink = sink.reshape(64, 2, 4, 128).transpose(0, 2, 1, 3)
     return nxt.reshape(256, 4, 128), sink.reshape(8, 8, 4, 256)
 

time: 28.3 us -> 27.1 us (0.958)
  Pallas kernels: 26.9 us -> 25.6 us
    pallas_call x1, Pallas kernels: 2.31 us -> 1.17 us  [on_device(): pl.pallas_call(finish, out_shape=(jax.ShapeDtypeStruct((1024, 128), F32),...]
where the time goes in v3:
time: 27.1 us; the launch traced here: 26.9 us
  Pallas kernels  25.6 us (94%)
  between operations  1.29 us (5%)
    pallas_call x1, Pallas kernels, on_device(): pl.pallas_call(exchange, out_shape=(vm((1024, 128), F32), vm((1024, 128),...  24.5 us
    pallas_call x1, Pallas kernels, on_device(): pl.pallas_call(finish, out_shape=(jax.ShapeDtypeStruct((1024, 128), F32),...  1.17 us

profile of v3, /device:TPU:1, one launch (start us, length us, event | category | flops | bytes accessed | tf_op | source)
XLA Modules:
  0.0 26.9 jit_solution(9741831725346079673)
XLA Ops:
  1.3 24.5 %shard_map.95 = (f32[1024,128]{1,0:T(8,128)S(1)}, f32[1024,128]{1,0:T(8,128)S(1)}, bf16[384,256]{1,0:T(8,128)(2,1)S(1)}, f32[512,128]{1,0:T(8,128)S(1)}, f32[128,1,128]{2,1,0:T(1,128)S(1)}) custom-call(f32[512,128]{1,0:T(8,128)} %bitcast.18, f32[1024,128]{1,0:T(8,128)} %bitcast.16, f32[1024,128]{1,0:T(8,128)} %bitcast.17, f32[4,256]{1,0:T(4,128)} %bitcast.19, ...), custom_call_target="tpu_custom_call" | custom-call | tf_op jit(solution)/shard_map/pallas_call | solution.py:307
  25.8 1.2 %shard_map.96 = (f32[1024,128]{1,0:T(8,128)}, f32[512,128]{1,0:T(8,128)}) custom-call(f32[1024,128]{1,0:T(8,128)S(1)} %get-tuple-element.9.pm, f32[1024,128]{1,0:T(8,128)S(1)} %get-tuple-element.10.um, bf16[384,256]{1,0:T(8,128)(2,1)S(1)} %get-tuple-element.11.sel, f32[512,128]{1,0:T(8,128)S(1)} %get-tuple-element.12.sink, ...), custom_call_target="tpu_custom_call" | custom-call | tf_op jit(solution)/shard_map/pallas_call | solution.py:333

commit v4 on v3

--- a/solution.py
+++ b/solution.py
@@ -101,8 +101,6 @@
         return (x + o[0]) & 3, (y + o[1]) & 3, c ^ o[2]
 
     barrier = pltpu.get_barrier_semaphore()
-    for dz in (2, 1, 3):
-        pl.semaphore_signal(barrier, inc=1, device_id=device(x, y, (z + dz) & 3, c), device_id_type=MESH)
     for o in PLANE:
         ox, oy, oc = beside(o)
         pl.semaphore_signal(barrier, inc=1, device_id=device(ox, oy, z, oc), device_id_type=MESH)
@@ -114,7 +112,7 @@
         def copy_to(x, y, c):
             there = place(x, y, p, c)
             return pltpu.make_async_remote_copy(
-                src.at[rows(there)], dst.at[rows(me)], send_s, recv_s.at[z],
+                src.at[rows(there)], dst.at[rows(me)], send_s, recv_s,
                 device_id=device(x, y, p, c), device_id_type=MESH,
             )
 
@@ -127,7 +125,7 @@
 
         @pl.when(z == p)
         def _():
-            pltpu.make_async_copy(src.at[rows(me)], dst.at[rows(me)], recv_s.at[z]).start()
+            pltpu.make_async_copy(src.at[rows(me)], dst.at[rows(me)], recv_s).start()
 
     def block(r):
         return pl.ds(8 * r, MESSAGE)
@@ -167,11 +165,18 @@
     )
 
     def tell():
-        pl.semaphore_wait(barrier, len(PLANE) + 3)
-        for dz in (2, 1, 3):
-            pl.semaphore_signal(plane_sem.at[z], inc=1, device_id=device(x, y, (z + dz) & 3, c), device_id_type=MESH)
-
-    late = (x >= 2) & (y >= 2) & (z >= 2)
+        pl.semaphore_wait(barrier, len(PLANE) + z)
+        for dz in (1, 2, 3):
+
+            @pl.when(z >= dz)
+            def _():
+                pl.semaphore_signal(plane_sem.at[z], inc=1, device_id=device(x, y, z - dz, c), device_id_type=MESH)
+
+            @pl.when(z + dz < 4)
+            def _():
+                pl.semaphore_signal(barrier, inc=1, device_id=device(x, y, z + dz, c), device_id_type=MESH)
+
+    late = (x >= 1) & (y >= 1)
     pl.when(late)(tell)
 
     zero, one = jnp.zeros((8, 128), F32), jnp.ones((8, 128), F32)
@@ -216,34 +221,87 @@
         halves = [[rb[pl.ds(256 * p + 2 * k + half, 32, stride=8), :] for k in range(CAP)] for half in range(2)]
         return split2(jnp.concatenate([jnp.concatenate(half + blank, axis=0) for half in halves], axis=1))
 
+    def whole():
+        lax.fori_loop(0, SUB // 2, lambda i, d: d + double_step(pm, cm, 0, zero, uptake), zero)
+
+    @pl.when((z == 0) & (x < 2) & (y < 2))
+    def _():
+        whole()
+
     pl.when(jnp.logical_not(late))(tell)
 
     def give(p):
-        @pl.when(z != p)
+        @pl.when(z < p)
         def _():
             pl.semaphore_wait(plane_sem.at[p], 1)
 
-        send(p, sb, rb, send_sem, recv_sem, block)
-
-    def answer(p):
-        view = rb.at[pl.ds(0, 32 * MESSAGE), :]
-        pltpu.make_async_copy(view, view, recv_sem.at[p]).wait()
+        send(p, sb, rb, send_sem, recv_sem.at[2 * z + jnp.minimum(y, 1)], block)
+
+    def take(p, part):
+        view = rb.at[pl.ds(0, (8, 24)[part] * MESSAGE), :]
+        pltpu.make_async_copy(view, view, recv_sem.at[2 * p + part]).wait()
+
+    def values_of(info, high, mid):
+        field = dot(soil_high, high, NT) + dot(soil_high, mid, NT) + dot(soil_mid, high, NT)
+        masked = jnp.where(tiles == info[0:1], field, 0.0)
+        return [jnp.sum(masked[64 * f : 64 * f + 64], axis=0, keepdims=True) for f in range(4)]
+
+    def items_of(start, n):
+        items = rb[pl.ds(start + 6, n, stride=8), :]
+        rest = jnp.full((128 - 3 * n, 128), -1.0, F32)
+        return jnp.concatenate([items, pltpu.roll(items, 96, 1), pltpu.roll(items, 64, 1), rest], axis=0).T
+
+    def by_source(values, n):
+        reply = jnp.concatenate(values + [jnp.zeros((124, 128), F32)], axis=0).T
+        return reply[0:n] + pltpu.roll(reply[n : 2 * n], 8, 1) + pltpu.roll(reply[2 * n : 3 * n], 16, 1)
+
+    def reply_to(y_there):
+        for x_there in (0, 1, 3, 2):
+            for c_there in range(2):
+                there = place(x_there, y_there, 0, c_there)
+                pltpu.make_async_remote_copy(
+                    qb.at[there], ret.at[me], send2_sem, recv2_sem.at[z],
+                    device_id=device(x_there, y_there, 0, c_there), device_id_type=MESH,
+                ).start()
+
+    def answer_first():
+        take(0, 0)
+        blank = [jnp.zeros((104, 128), F32)]
+        halves = [[rb[pl.ds(2 * k + half, 8, stride=8), :] for k in range(CAP)] for half in range(2)]
+        high, mid = split2(jnp.concatenate([jnp.concatenate(half + blank, axis=0) for half in halves], axis=1))
+        qb[pl.ds(0, 8), 0, :] = by_source(values_of(items_of(0, 8), high, mid), 8)
+        reply_to(0)
+
+    def answer(p, first=True):
+        if first:
+            take(p, 0)
+        take(p, 1)
         high, mid = arrived(p)
-        field = dot(soil_high, high, NT) + dot(soil_high, mid, NT) + dot(soil_mid, high, NT)
-        items = rb[pl.ds(256 * p + 6, 32, stride=8), :]
-        info = jnp.concatenate(
-            [items, pltpu.roll(items, 96, 1), pltpu.roll(items, 64, 1), jnp.full((32, 128), -1.0, F32)], axis=0
-        ).T
-        masked = jnp.where(tiles == info[0:1], field, 0.0)
-        values = [jnp.sum(masked[64 * f : 64 * f + 64], axis=0, keepdims=True) for f in range(4)]
-        reply = jnp.concatenate(values + [jnp.zeros((124, 128), F32)], axis=0).T
-        qb[pl.ds(32 * p, 32), 0, :] = reply[0:32] + pltpu.roll(reply[32:64], 8, 1) + pltpu.roll(reply[64:96], 16, 1)
-        send(p, qb, ret, send2_sem, recv2_sem, lambda r: r)
+        info = items_of(256 * p, 32)
+        values = values_of(info, high, mid)
+        reply = by_source(values, 32)
+        if first:
+            qb[pl.ds(32 * p, 32), 0, :] = reply
+            send(p, qb, ret, send2_sem, recv2_sem.at[z], lambda r: r)
+        else:
+            qb[pl.ds(8, 24), 0, :] = reply[8:32]
+            for y_there in (1, 3, 2):
+                reply_to(y_there)
         info_v[pl.ds(24 * p, 24), :] = jnp.concatenate([info[0:12]] + values + [jnp.zeros((8, 128), F32)], axis=0)
 
     for p in range(4):
         give(p)
-    for p in range(4):
+
+    @pl.when(z < 2)
+    def _():
+        answer(0)
+
+    @pl.when(z >= 2)
+    def _():
+        answer_first()
+        answer(0, False)
+
+    for p in range(1, 4):
         answer(p)
 
     sink = jnp.zeros((256, 256), F32)
@@ -257,7 +315,10 @@
     for f in range(4):
         for half in range(2):
             sink_v[pl.ds(4 * half + f, 64, stride=8), :] = sink[64 * f : 64 * f + 64, 128 * half : 128 * half + 128]
-    lax.fori_loop(0, SUB // 2, lambda i, d: d + double_step(pm, cm, 0, zero, uptake), zero)
+    @pl.when(jnp.logical_not((z == 0) & (x < 2) & (y < 2)))
+    def _():
+        whole()
+
 
     for p in range(4):
         view = ret.at[pl.ds(0, 32)]
@@ -315,7 +376,7 @@
             vm((512, 128), F32), vm((1024, 128), F32), vm((1024, 128), F32), vm((4, 256), F32), vm((256, 256), F32),
             vm((1, 256), jnp.int32), vm((1, 256), jnp.int32), vm((1024, 128), F32), vm((1024, 128), F32),
             vm((1024, 128), F32), vm((1024, 128), F32), vm((128, 1, 128), F32), vm((96, 128), F32),
-            dma((7,)), pltpu.SemaphoreType.REGULAR((4,)), dma(()), dma((4,)), dma(()), dma((4,)),
+            dma((7,)), pltpu.SemaphoreType.REGULAR((4,)), dma(()), dma((8,)), dma(()), dma((4,)),
         ],
         compiler_params=pltpu.CompilerParams(
             collective_id=0, has_side_effects=True, vmem_limit_bytes=32 * 1024 * 1024

time: 27.1 us -> 26.7 us (0.985)
  Pallas kernels: 25.6 us -> 25.3 us
    pallas_call x1, Pallas kernels: 24.5 us -> 24.2 us  [on_device(): pl.pallas_call(exchange, out_shape=(vm((1024, 128), F32), vm((1024, 128),...]
where the time goes in v4:
time: 26.7 us; the launch traced here: 26.6 us
  Pallas kernels  25.3 us (95%)
  between operations  1.29 us (5%)
    pallas_call x1, Pallas kernels, on_device(): pl.pallas_call(exchange, out_shape=(vm((1024, 128), F32), vm((1024, 128),...  24.2 us
    pallas_call x1, Pallas kernels, on_device(): pl.pallas_call(finish, out_shape=(jax.ShapeDtypeStruct((1024, 128), F32),...  1.17 us

profile of v4, /device:TPU:1, one launch (start us, length us, event | category | flops | bytes accessed | tf_op | source)
XLA Modules:
  0.0 26.6 jit_solution(8566489320225014156)
XLA Ops:
  1.3 24.2 %shard_map.95 = (f32[1024,128]{1,0:T(8,128)S(1)}, f32[1024,128]{1,0:T(8,128)S(1)}, bf16[384,256]{1,0:T(8,128)(2,1)S(1)}, f32[512,128]{1,0:T(8,128)S(1)}, f32[128,1,128]{2,1,0:T(1,128)S(1)}) custom-call(f32[512,128]{1,0:T(8,128)} %bitcast.18, f32[1024,128]{1,0:T(8,128)} %bitcast.16, f32[1024,128]{1,0:T(8,128)} %bitcast.17, f32[4,256]{1,0:T(4,128)} %bitcast.19, ...), custom_call_target="tpu_custom_call" | custom-call | tf_op jit(solution)/shard_map/pallas_call | solution.py:368
  25.4 1.2 %shard_map.96 = (f32[1024,128]{1,0:T(8,128)}, f32[512,128]{1,0:T(8,128)}) custom-call(f32[1024,128]{1,0:T(8,128)S(1)} %get-tuple-element.9.pm, f32[1024,128]{1,0:T(8,128)S(1)} %get-tuple-element.10.um, bf16[384,256]{1,0:T(8,128)(2,1)S(1)} %get-tuple-element.11.sel, f32[512,128]{1,0:T(8,128)S(1)} %get-tuple-element.12.sink, ...), custom_call_target="tpu_custom_call" | custom-call | tf_op jit(solution)/shard_map/pallas_call | solution.py:394

commit v5 on v4

--- a/solution.py
+++ b/solution.py
@@ -205,17 +205,6 @@
     sb[pl.ds(6, 128, stride=8), :] = meta
 
 
-    loads[6].wait()
-    soil = jnp.concatenate(
-        [
-            jnp.concatenate([soil_v[pl.ds(4 * half + f, 64, stride=8), :] for half in range(2)], axis=1)
-            for f in range(4)
-        ],
-        axis=0,
-    )
-    soil_high, soil_mid = split2(soil)
-    tiles = (lax.broadcasted_iota(jnp.int32, (256, 128), 0) & 63).astype(F32)
-
     def arrived(p):
         blank = [jnp.zeros((32, 128), F32)]
         halves = [[rb[pl.ds(256 * p + 2 * k + half, 32, stride=8), :] for k in range(CAP)] for half in range(2)]
@@ -291,6 +280,17 @@
 
     for p in range(4):
         give(p)
+
+    loads[6].wait()
+    soil = jnp.concatenate(
+        [
+            jnp.concatenate([soil_v[pl.ds(4 * half + f, 64, stride=8), :] for half in range(2)], axis=1)
+            for f in range(4)
+        ],
+        axis=0,
+    )
+    soil_high, soil_mid = split2(soil)
+    tiles = (lax.broadcasted_iota(jnp.int32, (256, 128), 0) & 63).astype(F32)
 
     @pl.when(z < 2)
     def _():

time: 26.7 us -> 26.7 us (level)
  no operation moved by 1% of the time
where the time goes in v5:
time: 26.7 us; the launch traced here: 26.6 us
  Pallas kernels  25.3 us (95%)
  between operations  1.29 us (5%)
    pallas_call x1, Pallas kernels, on_device(): pl.pallas_call(exchange, out_shape=(vm((1024, 128), F32), vm((1024, 128),...  24.1 us
    pallas_call x1, Pallas kernels, on_device(): pl.pallas_call(finish, out_shape=(jax.ShapeDtypeStruct((1024, 128), F32),...  1.17 us

profile of v5, /device:TPU:1, one launch (start us, length us, event | category | flops | bytes accessed | tf_op | source)
XLA Modules:
  0.0 26.6 jit_solution(15360713529633462748)
XLA Ops:
  1.3 24.1 %shard_map.95 = (f32[1024,128]{1,0:T(8,128)S(1)}, f32[1024,128]{1,0:T(8,128)S(1)}, bf16[384,256]{1,0:T(8,128)(2,1)S(1)}, f32[512,128]{1,0:T(8,128)S(1)}, f32[128,1,128]{2,1,0:T(1,128)S(1)}) custom-call(f32[512,128]{1,0:T(8,128)} %bitcast.18, f32[1024,128]{1,0:T(8,128)} %bitcast.16, f32[1024,128]{1,0:T(8,128)} %bitcast.17, f32[4,256]{1,0:T(4,128)} %bitcast.19, ...), custom_call_target="tpu_custom_call" | custom-call | tf_op jit(solution)/shard_map/pallas_call | solution.py:368
  25.4 1.2 %shard_map.96 = (f32[1024,128]{1,0:T(8,128)}, f32[512,128]{1,0:T(8,128)}) custom-call(f32[1024,128]{1,0:T(8,128)S(1)} %get-tuple-element.9.pm, f32[1024,128]{1,0:T(8,128)S(1)} %get-tuple-element.10.um, bf16[384,256]{1,0:T(8,128)(2,1)S(1)} %get-tuple-element.11.sel, f32[512,128]{1,0:T(8,128)S(1)} %get-tuple-element.12.sink, ...), custom_call_target="tpu_custom_call" | custom-call | tf_op jit(solution)/shard_map/pallas_call | solution.py:394

commit v6 on v5

--- a/solution.py
+++ b/solution.py
@@ -166,11 +166,13 @@
 
     def tell():
         pl.semaphore_wait(barrier, len(PLANE) + z)
-        for dz in (1, 2, 3):
+        for dz in (3, 2, 1):
 
             @pl.when(z >= dz)
             def _():
                 pl.semaphore_signal(plane_sem.at[z], inc=1, device_id=device(x, y, z - dz, c), device_id_type=MESH)
+
+        for dz in (1, 2, 3):
 
             @pl.when(z + dz < 4)
             def _():

time: 26.7 us -> 26.7 us (level)
  no operation moved by 1% of the time
where the time goes in v6:
time: 26.7 us; the launch traced here: 26.6 us
  Pallas kernels  25.3 us (95%)
  between operations  1.29 us (5%)
    pallas_call x1, Pallas kernels, on_device(): pl.pallas_call(exchange, out_shape=(vm((1024, 128), F32), vm((1024, 128),...  24.2 us
    pallas_call x1, Pallas kernels, on_device(): pl.pallas_call(finish, out_shape=(jax.ShapeDtypeStruct((1024, 128), F32),...  1.17 us

profile of v6, /device:TPU:1, one launch (start us, length us, event | category | flops | bytes accessed | tf_op | source)
XLA Modules:
  0.0 26.6 jit_solution(10154310034337714129)
XLA Ops:
  1.3 24.2 %shard_map.95 = (f32[1024,128]{1,0:T(8,128)S(1)}, f32[1024,128]{1,0:T(8,128)S(1)}, bf16[384,256]{1,0:T(8,128)(2,1)S(1)}, f32[512,128]{1,0:T(8,128)S(1)}, f32[128,1,128]{2,1,0:T(1,128)S(1)}) custom-call(f32[512,128]{1,0:T(8,128)} %bitcast.18, f32[1024,128]{1,0:T(8,128)} %bitcast.16, f32[1024,128]{1,0:T(8,128)} %bitcast.17, f32[4,256]{1,0:T(4,128)} %bitcast.19, ...), custom_call_target="tpu_custom_call" | custom-call | tf_op jit(solution)/shard_map/pallas_call | solution.py:370
  25.4 1.2 %shard_map.96 = (f32[1024,128]{1,0:T(8,128)}, f32[512,128]{1,0:T(8,128)}) custom-call(f32[1024,128]{1,0:T(8,128)S(1)} %get-tuple-element.9.pm, f32[1024,128]{1,0:T(8,128)S(1)} %get-tuple-element.10.um, bf16[384,256]{1,0:T(8,128)(2,1)S(1)} %get-tuple-element.11.sel, f32[512,128]{1,0:T(8,128)S(1)} %get-tuple-element.12.sink, ...), custom_call_target="tpu_custom_call" | custom-call | tf_op jit(solution)/shard_map/pallas_call | solution.py:396
